TPU v7x, 32 devices: a whole 2x2x4 slice. The times are simulated.
32 devices in a mesh: row: 4 (over x, core), col: 8 (over z, y).
Axes of the slice: x: 2, y: 2, z: 4, core: 2. Of those that a mesh axis runs over, the one named last changes fastest.
Arguments:
- states: bfloat16 [4096, 384], P(('row', 'col')), may hold values from -6 to 6
- mix_weight: bfloat16 [384, 384], replicated, may hold values from -0.3125 to 0.3125
- coherence: bfloat16 [4, 8, 32, 128, 128], P('row', 'col'), may hold values from -0.125 to 0.125
- block_row: int32 [4, 8, 32], P('row', 'col'), may hold values from 0 to 3, as said below
- block_col: int32 [4, 8, 32], P('row', 'col'), may hold values from 0 to 3
- block_count: int32 [4, 8], P('row', 'col'), may hold values from 8 to 32, as said below
- gain: float32 [384], replicated, may hold values from 0.5 to 1.5
- bias: float32 [384], replicated, may hold values from -3 to 3
Outputs:
- linked: bfloat16 [4096, 384], P(('row', 'col'))
Inputs may be any that keep to these rules, and one draw needn't show every extreme that they name: `block_count`: no device has more than 32 live slots, and some device has exactly 32. `block_row`: at most 8 of one device's slots name any one block row; in each column group some block row is named by 8 live slots of every device.
All inputs are finite; a program needn't handle non-finite values.
Results may differ from a plain program's by a relative error of at most 0.014.
Values may be sent and summed in bfloat16 or wider, within the bound.
A program may use at most 64 MiB of HBM per device.

v0:
```python
import jax
import jax.numpy as jnp
from jax import lax
from jax.sharding import PartitionSpec as P

ITERS = 2


def normalize(hidden, coupled, gain, bias):
    summed_in = hidden.astype(jnp.float32) + coupled
    mean_value = jnp.mean(summed_in, axis=-1, keepdims=True)
    centered = summed_in - mean_value
    variance = jnp.mean(centered * centered, axis=-1, keepdims=True)
    return (centered * lax.rsqrt(variance + 1e-05) * gain + bias).astype(jnp.bfloat16)


def to_grid(values):
    return lax.all_to_all(values, "col", split_axis=0, concat_axis=0, tiled=True)


def seat_layout(blocks, row_ids, col_ids, live_count, row_groups, seats_per_row):
    slot_total = row_ids.shape[0]
    block_len = blocks.shape[1]
    slot_ids = jnp.arange(slot_total, dtype=jnp.int32)
    live_mask = slot_ids < live_count
    earlier = (
        (row_ids[:, None] == row_ids[None, :])
        & (slot_ids[None, :] < slot_ids[:, None])
        & live_mask[None, :]
    )
    rank_in_row = jnp.sum(earlier.astype(jnp.int32), axis=1)
    seat_total = row_groups * seats_per_row
    seat_index = jnp.where(live_mask, row_ids * seats_per_row + rank_in_row, seat_total)
    seat_blocks = (
        jnp.zeros((seat_total, block_len, block_len), blocks.dtype)
        .at[seat_index]
        .set(blocks, mode="drop")
    )
    seat_cols = jnp.zeros((seat_total,), jnp.int32).at[seat_index].set(col_ids, mode="drop")
    return (
        seat_blocks.reshape(row_groups, seats_per_row, block_len, block_len),
        seat_cols.reshape(row_groups, seats_per_row),
    )


def seat_product(seat_blocks, seat_cols, pieces_all):
    pieces = pieces_all[seat_cols]
    return jnp.einsum("skab,skbh->sah", seat_blocks, pieces, preferred_element_type=jnp.float32)


def couple(grid_mixed, prepared):
    gathered = lax.all_gather(grid_mixed, "row", axis=0, tiled=True)
    row_groups = lax.axis_size("row")
    block_len = grid_mixed.shape[0]
    feat_width = grid_mixed.shape[1]
    pieces_all = gathered.reshape(row_groups, block_len, feat_width)
    seat_blocks, seat_cols = prepared
    flat_sum = seat_product(seat_blocks, seat_cols, pieces_all).reshape(
        row_groups * block_len, feat_width
    )
    return lax.psum_scatter(
        flat_sum.astype(jnp.bfloat16), "row", scatter_dimension=0, tiled=True
    ).astype(jnp.float32)


def body(states, mix_weight, coherence, block_row, block_col, block_count, gain, bias):
    blocks = coherence[0, 0]
    row_ids = block_row[0, 0]
    col_ids = block_col[0, 0]
    live_count = block_count[0, 0]
    row_groups = lax.axis_size("row")
    slot_total = row_ids.shape[0]
    seats_per_row = max(2, (slot_total + row_groups - 1) // row_groups)
    prepared = seat_layout(blocks, row_ids, col_ids, live_count, row_groups, seats_per_row)
    hidden = states
    for iteration in range(ITERS):
        mixed = jnp.dot(hidden, mix_weight, preferred_element_type=jnp.float32).astype(jnp.bfloat16)
        coupled = couple(to_grid(mixed), prepared)
        coupled = lax.all_to_all(
            coupled.astype(jnp.bfloat16), "col", split_axis=0, concat_axis=0, tiled=True
        ).astype(coupled.dtype)
        hidden = normalize(hidden, coupled, gain, bias)
    return hidden


def solution(mesh):
    placed = (
        P(("row", "col"), None),
        P(),
        P("row", "col", None, None, None),
        P("row", "col", None),
        P("row", "col", None),
        P("row", "col"),
        P(),
        P(),
    )
    return jax.shard_map(
        body, mesh=mesh, in_specs=placed, out_specs=P(("row", "col"), None), check_vma=False
    )
```

profile of v0, /device:TPU:0, one launch (start us, length us, event | category | flops | bytes accessed | tf_op | source)
XLA Modules:
  0.0 131.8 jit_solution(14854087757491817840)
XLA Ops:
  6.5 0.0 copy-start
  6.5 1.0 copy-done
  7.5 1.7 %convolution_convert_fusion.1 = bf16[128,384]{1,0:T(8,128)(2,1)} fusion(bf16[128,384]{1,0:T(8,128)(2,1)} %param.8, bf16[384,384]{1,0:T(8,128)(2,1)S(1)} %copy-done), kind=kOutput, calls=%fused_computation.9 | convolution fusion | flops 37797888 | bytes 491520 | tf_op jit(solution)/shard_map/dot_general | solution.py:77
  9.2 7.3 %all-to-all-start = ((bf16[8,16,384]{2,1,0:T(8,128)(2,1)}), bf16[8,16,384]{2,1,0:T(8,128)(2,1)S(1)}, u32[]{:S(2)}, u32[]{:S(2)}) async-start(bf16[8,16,384]{2,1,0:T(8,128)(2,1)} %bitcast.7), calls=%async_computation | async-start | bytes 196608 | tf_op jit(solution)/shard_map/all_to_all | solution.py:18
  16.5 0.0 reduce-scatter.3.cloned.1.call-start
  17.2 0.9 convert_reduce_fusion
  18.1 0.7 fusion.8
  18.8 0.8 scatter_custom_fusion.1
  19.6 0.1 reshape.128
  19.7 0.1 reshape.134
  19.8 0.2 broadcast_in_dim.6
  20.0 3.6 %scatter_fusion = bf16[32,128,128]{2,1,0:T(8,128)(2,1)S(1)} fusion(bf16[32,128,128]{2,1,0:T(8,128)(2,1)S(1)} %broadcast_in_dim.6, s32[32]{0:T(128)S(1)} %fusion.8, bf16[32,128,128]{2,1,0:T(8,128)(2,1)} %bitcast.71), kind=kCustom, calls=%fused_computation.2 | custom fusion | bytes 3145856 | tf_op jit(solution)/shard_map/scatter | solution.py:37
  23.7 0.0 all-to-all-done
  23.7 6.5 %all_gather.6 = bf16[512,384]{1,0:T(8,128)(2,1)S(1)} all-gather(bf16[128,384]{1,0:T(8,128)(2,1)S(1)} %bitcast.72), channel_id=1, replica_groups=mesh['row'=4,'col'=8] {'row'}, dimensions={0}, use_global_device_ids=true | all-gather | bytes 491520 | tf_op jit(solution)/shard_map/all_gather | solution.py:52
  30.1 2.6 %gather_fusion = bf16[32,128,384]{2,1,0:T(8,128)(2,1)} fusion(bf16[4,128,384]{2,1,0:T(8,128)(2,1)S(1)} %bitcast.64, s32[1024]{0:T(1024)S(1)} %pad_clamp_fusion), kind=kCustom, calls=%fused_computation | custom fusion | bytes 6291584 | tf_op jit(solution)/shard_map/gather | solution.py:47
  32.8 0.0 copy-start.1
  32.8 0.0 copy-start.2
  32.8 0.0 copy-start.3
  32.8 3.4 %fusion = bf16[4,128,384]{2,1,0:T(8,128)(2,1)} fusion(bf16[4,8,128,128]{3,2,1,0:T(8,128)(2,1)S(1)} %bitcast.65, bf16[4,8,128,384]{3,2,1,0:T(8,128)(2,1)} %bitcast.68), kind=kOutput, calls=%fused_computation.6 | convolution fusion | flops 402849792 | bytes 4587520 | tf_op jit(solution)/shard_map/skab,skbh->sah/dot_general | solution.py:48
  36.2 0.0 reduce-scatter.3.cloned.1.call-update
  36.2 0.0 reduce-scatter.5.cloned.1.call-start
  36.2 22.0 %reduce-scatter.3.cloned.1.call-done = bf16[128,384]{1,0:T(8,128)(2,1)} async-done(((bf16[512,384]{1,0:T(8,128)(2,1)}), bf16[128,384]{1,0:T(8,128)(2,1)}) %reduce-scatter.3.cloned.1.call-update) | async-done | bytes 98320 | tf_op jit(solution)/shard_map/reduce_scatter | solution.py:61
  58.2 12.6 %all_to_all.42 = bf16[8,16,384]{2,1,0:T(8,128)(2,1)S(1)} all-to-all(bf16[8,16,384]{2,1,0:T(8,128)(2,1)} %bitcast.75), channel_id=1, replica_groups=mesh['row'=4,'col'=8] {'col'}, dimensions={0} | all-to-all | bytes 196608 | tf_op jit(solution)/shard_map/all_to_all | solution.py:79
  70.9 0.0 copy-done.1
  70.9 0.1 fusion.3
  71.0 0.2 multiply_reduce_fusion.1
  71.2 0.0 copy-done.2
  71.2 0.0 copy-done.3
  71.2 0.1 add_convert_fusion.1
  71.4 0.2 convolution_convert_fusion
  71.6 9.5 %all_to_all.43 = bf16[8,16,384]{2,1,0:T(8,128)(2,1)S(1)} all-to-all(bf16[8,16,384]{2,1,0:T(8,128)(2,1)S(1)} %bitcast.74), channel_id=1, replica_groups=mesh['row'=4,'col'=8] {'col'}, dimensions={0} | all-to-all | bytes 196608 | tf_op jit(solution)/shard_map/all_to_all | solution.py:18
  81.1 6.1 %all_gather.7 = bf16[512,384]{1,0:T(8,128)(2,1)S(1)} all-gather(bf16[128,384]{1,0:T(8,128)(2,1)S(1)} %bitcast.73), channel_id=1, replica_groups=mesh['row'=4,'col'=8] {'row'}, dimensions={0}, use_global_device_ids=true | all-gather | bytes 491520 | tf_op jit(solution)/shard_map/all_gather | solution.py:52
  87.2 2.6 %gather_fusion.1 = bf16[32,128,384]{2,1,0:T(8,128)(2,1)} fusion(bf16[4,128,384]{2,1,0:T(8,128)(2,1)S(1)} %bitcast.63, s32[1024]{0:T(1024)S(1)} %pad_clamp_fusion), kind=kCustom, calls=%fused_computation.1 | custom fusion | bytes 6291584 | tf_op jit(solution)/shard_map/gather | solution.py:47
  89.9 3.3 %fusion.1 = bf16[4,128,384]{2,1,0:T(8,128)(2,1)} fusion(bf16[4,8,128,128]{3,2,1,0:T(8,128)(2,1)S(1)} %bitcast.66, bf16[4,8,128,384]{3,2,1,0:T(8,128)(2,1)} %bitcast.67), kind=kOutput, calls=%fused_computation.7 | convolution fusion | flops 402849792 | bytes 4587520 | tf_op jit(solution)/shard_map/skab,skbh->sah/dot_general | solution.py:48
  93.2 0.0 reduce-scatter.5.cloned.1.call-update
  93.2 18.0 %reduce-scatter.5.cloned.1.call-done = bf16[128,384]{1,0:T(8,128)(2,1)} async-done(((bf16[512,384]{1,0:T(8,128)(2,1)}), bf16[128,384]{1,0:T(8,128)(2,1)}) %reduce-scatter.5.cloned.1.call-update) | async-done | bytes 98320 | tf_op jit(solution)/shard_map/reduce_scatter | solution.py:61
  111.2 12.6 %all_to_all.44 = bf16[8,16,384]{2,1,0:T(8,128)(2,1)S(1)} all-to-all(bf16[8,16,384]{2,1,0:T(8,128)(2,1)} %bitcast.76), channel_id=1, replica_groups=mesh['row'=4,'col'=8] {'col'}, dimensions={0} | all-to-all | bytes 196608 | tf_op jit(solution)/shard_map/all_to_all | solution.py:79
  123.9 0.1 fusion.5
  124.0 0.2 multiply_reduce_fusion
  124.2 0.8 add_convert_fusion
  (7 shorter events, 0.0 us)
Async XLA Ops:
  6.5 1.0 copy-start
  9.2 14.4 %all-to-all-start = ((bf16[8,16,384]{2,1,0:T(8,128)(2,1)}), bf16[8,16,384]{2,1,0:T(8,128)(2,1)S(1)}, u32[]{:S(2)}, u32[]{:S(2)}) async-start(bf16[8,16,384]{2,1,0:T(8,128)(2,1)} %bitcast.7), calls=%async_computation | async-start | bytes 196608 | tf_op jit(solution)/shard_map/all_to_all | solution.py:18
  16.5 41.7 %reduce-scatter.3.cloned.1.call-start = ((), (), s32[]{:S(2)}) async-start(), calls=%async_computation.6 | async-start | bytes 491520 | tf_op jit(solution)/shard_map/reduce_scatter | solution.py:61
  32.8 38.1 %copy-start.1 = (bf16[128,384]{1,0:T(8,128)(2,1)S(1)}, bf16[128,384]{1,0:T(8,128)(2,1)}, u32[]{:S(2)}) copy-start(bf16[128,384]{1,0:T(8,128)(2,1)} %param.8) | copy-start | bytes 294916
  32.8 38.4 %copy-start.2 = (f32[384]{0:T(512)S(1)}, f32[384]{0:T(512)}, u32[]{:S(2)}) copy-start(f32[384]{0:T(512)} %param.15) | copy-start | bytes 4612
  32.8 38.4 %copy-start.3 = (f32[384]{0:T(512)S(1)}, f32[384]{0:T(512)}, u32[]{:S(2)}) copy-start(f32[384]{0:T(512)} %param.14) | copy-start | bytes 4612
  36.2 75.0 %reduce-scatter.5.cloned.1.call-start = ((), (), s32[]{:S(2)}) async-start(), calls=%async_computation.7 | async-start | bytes 491520 | tf_op jit(solution)/shard_map/reduce_scatter | solution.py:61
Sparse Core Ops, SparseCore 0:
  36.3 21.8 reduce-scatter.2
  93.4 17.8 reduce-scatter.4
where the time goes:
time: 132 us
  blocking collectives  47.4 us (36%)
  waiting for transfers between devices  40 us (30%)
  between operations  14.2 us (11%)
  local copies, waits for them, and re-layouts  11.1 us (8%)
  matrix products  8.67 us (7%)
  starting transfers between devices  7.36 us (6%)
  other arithmetic  3.09 us (2%)
    reduce_scatter x2, waiting for transfers between devices, couple(): lax.psum_scatter(flat_sum.astype(jnp.bfloat16), 'row', scatter_dimension=...  40 us
    all_to_all x2, blocking collectives, body(): lax.all_to_all(coupled.astype(jnp.bfloat16), 'col', split_axis=0, concat_...  25.3 us
    all_gather x2, blocking collectives, couple(): gathered = lax.all_gather(grid_mixed, 'row', axis=0, tiled=True)  12.6 us
    all_to_all x1, blocking collectives, to_grid(): lax.all_to_all(values, 'col', split_axis=0, concat_axis=0, tiled=True)  9.51 us
    all_to_all x1, starting transfers between devices, to_grid(): lax.all_to_all(values, 'col', split_axis=0, concat_axis=0, tiled=True)  7.28 us
    dot_general x2, matrix products, seat_product(): jnp.einsum('skab,skbh->sah', seat_blocks, pieces, preferred_element_type=...  6.72 us
    gather x2, local copies, waits for them, and re-layouts, seat_product(): pieces = pieces_all[seat_cols]  5.3 us
    scatter x1, local copies, waits for them, and re-layouts, seat_layout(): seat_blocks = jnp.zeros((seat_total, block_len, block_len), blocks.dtype)...  3.62 us
  transfers between devices with their start and end apart: 3, of which 2 were waited for; matrix products, arithmetic and copies ran while one was open for 5% of the time, Pallas kernels for 0%

commit v1 on v0

--- a/solution.py
+++ b/solution.py
@@ -1,9 +1,15 @@
+import functools
+
 import jax
 import jax.numpy as jnp
 from jax import lax
+from jax.experimental import pallas as pl
+from jax.experimental.pallas import tpu as pltpu
 from jax.sharding import PartitionSpec as P
 
 ITERS = 2
+ROW_TILE = 16
+MESH_IDS = pl.DeviceIdType.MESH
 
 
 def normalize(hidden, coupled, gain, bias):
@@ -43,44 +49,385 @@
     )
 
 
-def seat_product(seat_blocks, seat_cols, pieces_all):
-    pieces = pieces_all[seat_cols]
-    return jnp.einsum("skab,skbh->sah", seat_blocks, pieces, preferred_element_type=jnp.float32)
-
-
 def couple(grid_mixed, prepared):
     gathered = lax.all_gather(grid_mixed, "row", axis=0, tiled=True)
     row_groups = lax.axis_size("row")
-    block_len = grid_mixed.shape[0]
-    feat_width = grid_mixed.shape[1]
+    block_len, feat_width = grid_mixed.shape
     pieces_all = gathered.reshape(row_groups, block_len, feat_width)
     seat_blocks, seat_cols = prepared
-    flat_sum = seat_product(seat_blocks, seat_cols, pieces_all).reshape(
-        row_groups * block_len, feat_width
-    )
+    chosen = (seat_cols[:, :, None] == jnp.arange(row_groups)).astype(grid_mixed.dtype)
+    pieces = jnp.einsum(
+        "skj,jbh->skbh", chosen, pieces_all, preferred_element_type=jnp.float32
+    ).astype(grid_mixed.dtype)
+    flat_sum = jnp.einsum(
+        "skab,skbh->sah", seat_blocks, pieces, preferred_element_type=jnp.float32
+    ).reshape(row_groups * block_len, feat_width)
     return lax.psum_scatter(
         flat_sum.astype(jnp.bfloat16), "row", scatter_dimension=0, tiled=True
     ).astype(jnp.float32)
 
 
-def body(states, mix_weight, coherence, block_row, block_col, block_count, gain, bias):
-    blocks = coherence[0, 0]
+def general_body(states, mix_weight, coherence, block_row, block_col, block_count, gain, bias):
     row_ids = block_row[0, 0]
-    col_ids = block_col[0, 0]
-    live_count = block_count[0, 0]
     row_groups = lax.axis_size("row")
     slot_total = row_ids.shape[0]
     seats_per_row = max(2, (slot_total + row_groups - 1) // row_groups)
-    prepared = seat_layout(blocks, row_ids, col_ids, live_count, row_groups, seats_per_row)
-    hidden = states
+    prepared = seat_layout(
+        coherence[0, 0], row_ids, block_col[0, 0], block_count[0, 0], row_groups, seats_per_row
+    )
+    hidden = to_grid(states)
     for iteration in range(ITERS):
         mixed = jnp.dot(hidden, mix_weight, preferred_element_type=jnp.float32).astype(jnp.bfloat16)
-        coupled = couple(to_grid(mixed), prepared)
-        coupled = lax.all_to_all(
-            coupled.astype(jnp.bfloat16), "col", split_axis=0, concat_axis=0, tiled=True
-        ).astype(coupled.dtype)
-        hidden = normalize(hidden, coupled, gain, bias)
-    return hidden
+        hidden = normalize(hidden, couple(mixed, prepared), gain, bias)
+    return to_grid(hidden)
+
+
+def lowest_bit_index(bit):
+    index = jnp.int32(0)
+    for power, pattern in enumerate((-1431655766, -858993460, -252645136, -16711936, -65536)):
+        index = index + jnp.where((bit & jnp.int32(pattern)) != 0, jnp.int32(1 << power), jnp.int32(0))
+    return index
+
+
+def link_kernel(
+    n_col,
+    seats,
+    states,
+    mix_weight,
+    coherence,
+    row_ids_in,
+    col_ids_in,
+    live_count_in,
+    gain_in,
+    bias_in,
+    out,
+    row_ids,
+    col_ids,
+    live_count,
+    gain_row,
+    bias_row,
+    coh,
+    weight,
+    hall,
+    hall2,
+    fin,
+    near_out,
+    near_in,
+    far_part,
+    far_out,
+    far_in,
+    mate_out,
+    mate_in,
+    own_part,
+    joint,
+    load_sem,
+    a2a_send,
+    a2a_recv,
+    blk_send,
+    blk_recv,
+    xc_send,
+    xc_recv,
+    fw_send,
+    fw_recv,
+    mate_send,
+    mate_recv,
+    x2_send,
+    x2_recv,
+    m2_send,
+    m2_recv,
+    f2_send,
+    f2_recv,
+    back_send,
+    back_recv,
+):
+    r = lax.axis_index("row")
+    c = lax.axis_index("col")
+    blk = hall.shape[0] // 4
+    part = blk // n_col
+    slots = coh.shape[0]
+    mate = (r ^ 1, c)
+    across = (r ^ 2, c)
+
+    def remote(src, dst, send_sem, recv_sem, device):
+        return pltpu.make_async_remote_copy(
+            src_ref=src, dst_ref=dst, send_sem=send_sem, recv_sem=recv_sem,
+            device_id=device, device_id_type=MESH_IDS,
+        )
+
+    def rows_at(index, size=part):
+        return pl.ds(pl.multiple_of(index * size, size), size)
+
+    barrier = pltpu.get_barrier_semaphore()
+    for step in range(1, n_col):
+        pl.semaphore_signal(
+            barrier, inc=1, device_id=(r, lax.rem(c + step, n_col)), device_id_type=MESH_IDS
+        )
+    for peer in (mate, across):
+        pl.semaphore_signal(barrier, inc=1, device_id=peer, device_id_type=MESH_IDS)
+    loads = [
+        pltpu.make_async_copy(source, held, load_sem.at[4 + place])
+        for place, (source, held) in enumerate(
+            (
+                (row_ids_in, row_ids),
+                (col_ids_in, col_ids),
+                (live_count_in, live_count),
+                (gain_in, gain_row),
+                (bias_in, bias_row),
+            )
+        )
+    ]
+    for load in loads:
+        load.start()
+    load_coh = pltpu.make_async_copy(coherence, coh, load_sem.at[0])
+    load_weight = pltpu.make_async_copy(mix_weight, weight, load_sem.at[1])
+    load_own = pltpu.make_async_copy(states.at[rows_at(c)], hall.at[rows_at(c)], load_sem.at[2])
+    load_coh.start()
+    load_own.start()
+    load_weight.start()
+
+    pl.semaphore_wait(barrier, n_col + 1)
+
+    to_col = []
+    for step in range(1, n_col):
+        there = lax.rem(c + step, n_col)
+        copy = remote(
+            states.at[rows_at(there)], hall.at[rows_at(c)],
+            a2a_send.at[step], a2a_recv.at[step], (r, there),
+        )
+        copy.start()
+        to_col.append(copy)
+
+    def cross(step):
+        source = lax.rem(c + n_col - step, n_col)
+        here = hall.at[rows_at(source)]
+        slot2 = hall.at[pl.ds(pl.multiple_of(2 * blk + source * part, part), part)]
+        slot3 = hall.at[pl.ds(pl.multiple_of(3 * blk + source * part, part), part)]
+        over = remote(here, slot2, xc_send.at[step], xc_recv.at[step], across)
+        onward = remote(slot2, slot3, fw_send.at[step], fw_recv.at[step], mate)
+        return over, onward
+
+    load_own.wait()
+    crossings = [cross(step) for step in range(n_col)]
+    crossings[0][0].start()
+
+    for load in loads:
+        load.wait()
+    gain = gain_row[...].reshape(1, -1)
+    bias = bias_row[...].reshape(1, -1)
+    live = live_count[0, 0]
+    row_bits = [jnp.int32(0)] * 4
+    for k in range(slots):
+        named = row_ids[k]
+        bit = jnp.where(k < live, jnp.int32(1 << k if k < 31 else -(1 << 31)), jnp.int32(0))
+        for q in range(4):
+            row_bits[q] = row_bits[q] | jnp.where(named == (r ^ q), bit, jnp.int32(0))
+    load_coh.wait()
+
+    def partial(q, write):
+        target = r ^ q
+        bits = row_bits[q]
+        places, scales = [], []
+        for n in range(seats):
+            low = bits & (-bits)
+            place = lowest_bit_index(low)
+            named = jnp.where(low != 0, col_ids[place] ^ target, jnp.int32(-1))
+            places.append(place)
+            scales.append(
+                [jnp.where(named == t, jnp.float32(1), jnp.float32(0)) for t in range(4)]
+            )
+            bits = bits & (bits - 1)
+        size = 32
+
+        def some_rows(i, carry):
+            rows = rows_at(i, size)
+            sums = [jnp.zeros((size, blk), jnp.float32)] * 4
+            for n in range(seats):
+                block = coh[places[n], rows, :].astype(jnp.float32)
+                sums = [sums[t] + block * scales[n][t] for t in range(4)]
+            for t in range(4):
+                write(rows, t, sums[t])
+            return carry
+
+        lax.fori_loop(0, blk // size, some_rows, 0)
+
+    def into(ref):
+        def write(rows, t, values):
+            ref[rows, t * blk : (t + 1) * blk] = values.astype(ref.dtype)
+
+        return write
+
+    partial(3, into(near_out))
+    near = remote(near_out, near_in, blk_send.at[0], blk_recv.at[0], mate)
+    near.start()
+    partial(2, into(far_part))
+    near.wait_recv()
+    far_out[...] = (far_part[...] + near_in[...].astype(jnp.float32)).astype(far_out.dtype)
+    far = remote(far_out, far_in, blk_send.at[1], blk_recv.at[1], across)
+    far.start()
+    partial(1, into(mate_out))
+    mated = remote(mate_out, mate_in, blk_send.at[2], blk_recv.at[2], mate)
+    mated.start()
+    partial(0, into(own_part))
+
+    for step in range(1, n_col):
+        to_col[step - 1].wait_recv()
+        crossings[step][0].start()
+    own_block = remote(hall.at[pl.ds(0, blk)], hall.at[pl.ds(blk, blk)], mate_send, mate_recv, mate)
+    own_block.start()
+    for over, onward in crossings:
+        over.wait_recv()
+        onward.start()
+
+    mated.wait_recv()
+    far.wait_recv()
+    joint[...] = (
+        own_part[...]
+        + mate_in[...].astype(jnp.float32)
+        + far_in[...].astype(jnp.float32)
+    ).astype(joint.dtype)
+    load_weight.wait()
+    own_block.wait_recv()
+
+    def product(source, low, high):
+        return jnp.dot(
+            joint[:, low * blk : high * blk], source[low * blk : high * blk, :],
+            preferred_element_type=jnp.float32,
+        )
+
+    def settle(spread, source):
+        return source[0:blk, :], jnp.dot(
+            spread.astype(jnp.bfloat16), weight[...], preferred_element_type=jnp.float32
+        )
+
+    spread = product(hall, 0, 2)
+    for over, onward in crossings:
+        onward.wait_recv()
+    spread = spread + product(hall, 2, 4)
+    base, coupled = settle(spread, hall)
+
+    quarters = 4
+    size = blk // quarters
+    sent = []
+    for q in range(quarters):
+        low, high = q * size, (q + 1) * size
+        hall2[low:high, :] = normalize(base[low:high], coupled[low:high], gain, bias)
+        here = hall2.at[pl.ds(low, size)]
+        slot2 = hall2.at[pl.ds(2 * blk + low, size)]
+        slot3 = hall2.at[pl.ds(3 * blk + low, size)]
+        over = remote(here, slot2, x2_send.at[q], x2_recv.at[q], across)
+        over.start()
+        beside = remote(
+            here, hall2.at[pl.ds(blk + low, size)], m2_send.at[q], m2_recv.at[q], mate
+        )
+        beside.start()
+        onward = remote(slot2, slot3, f2_send.at[q], f2_recv.at[q], mate)
+        sent.append((over, beside, onward))
+    for over, beside, onward in sent:
+        beside.wait_recv()
+    spread = product(hall2, 0, 2)
+    for over, beside, onward in sent:
+        over.wait_recv()
+        onward.start()
+    spread = spread + product(hall2, 2, 3)
+    for over, beside, onward in sent:
+        onward.wait_recv()
+    spread = spread + product(hall2, 3, 4)
+    base, coupled = settle(spread, hall2)
+    fin[...] = normalize(base, coupled, gain, bias)
+
+    keep = pltpu.make_async_copy(fin.at[rows_at(c)], out.at[rows_at(c)], load_sem.at[3])
+    back = []
+    for step in range(1, n_col):
+        there = lax.rem(c + step, n_col)
+        copy = remote(
+            fin.at[rows_at(there)], out.at[rows_at(c)],
+            back_send.at[step], back_recv.at[step], (r, there),
+        )
+        copy.start()
+        back.append(copy)
+    keep.start()
+
+    for copy in to_col:
+        copy.wait_send()
+    for over, onward in crossings:
+        over.wait_send()
+        onward.wait_send()
+    for copy in (near, far, mated, own_block):
+        copy.wait_send()
+    for copies in sent:
+        for copy in copies:
+            copy.wait_send()
+    keep.wait()
+    for copy in back:
+        copy.wait_send()
+        copy.wait_recv()
+
+
+def kernel_body(states, mix_weight, coherence, block_row, block_col, block_count, gain, bias):
+    n_col = lax.axis_size("col")
+    row_groups = lax.axis_size("row")
+    blk, feat = states.shape
+    slots = coherence.shape[2]
+    seats = max(2, (slots + row_groups - 1) // row_groups)
+    any_space = pl.BlockSpec(memory_space=pl.ANY)
+    bf16, f32 = jnp.bfloat16, jnp.float32
+    dma = pltpu.SemaphoreType.DMA
+    wide = (blk, row_groups * blk)
+    return pl.pallas_call(
+        functools.partial(link_kernel, n_col, seats),
+        out_shape=jax.ShapeDtypeStruct((blk, feat), bf16),
+        in_specs=[any_space] * 8,
+        out_specs=OUT_SPACE,
+        scratch_shapes=[
+            pltpu.SMEM((slots,), jnp.int32),
+            pltpu.SMEM((slots,), jnp.int32),
+            pltpu.SMEM((1, 1), jnp.int32),
+            pltpu.VMEM((feat,), f32),
+            pltpu.VMEM((feat,), f32),
+            pltpu.VMEM((slots, blk, blk), bf16),
+            pltpu.VMEM((feat, feat), bf16),
+            pltpu.VMEM((row_groups * blk, feat), bf16),
+            pltpu.VMEM((row_groups * blk, feat), bf16),
+            pltpu.VMEM((blk, feat), bf16),
+            pltpu.VMEM(wide, bf16),
+            pltpu.VMEM(wide, bf16),
+            pltpu.VMEM(wide, f32),
+            pltpu.VMEM(wide, bf16),
+            pltpu.VMEM(wide, bf16),
+            pltpu.VMEM(wide, bf16),
+            pltpu.VMEM(wide, bf16),
+            pltpu.VMEM(wide, f32),
+            pltpu.VMEM(wide, bf16),
+            dma((9,)),
+            dma((n_col,)),
+            dma((n_col,)),
+            dma((3,)),
+            dma((3,)),
+            dma((n_col,)),
+            dma((n_col,)),
+            dma((n_col,)),
+            dma((n_col,)),
+            dma,
+            dma,
+        ]
+        + [dma((4,))] * 6
+        + [dma((n_col,))] * 2,
+        compiler_params=pltpu.CompilerParams(
+            collective_id=0, has_side_effects=True, vmem_limit_bytes=60 << 20
+        ),
+    )(
+        states,
+        mix_weight,
+        coherence.reshape(coherence.shape[2:]),
+        block_row.reshape(slots),
+        block_col.reshape(slots),
+        block_count,
+        gain,
+        bias,
+    )
+
+
+OUT_SPACE = pl.BlockSpec(memory_space=pltpu.VMEM)
 
 
 def solution(mesh):
@@ -94,6 +441,16 @@
         P(),
         P(),
     )
+    n_row, n_col = mesh.shape["row"], mesh.shape["col"]
+
+    def body(*args):
+        blk = args[0].shape[0]
+        slots = args[2].shape[2]
+        in_tiles = blk % n_col == 0 and (blk // n_col) % ROW_TILE == 0
+        if n_row == 4 and n_col > 1 and in_tiles and slots <= 32:
+            return kernel_body(*args)
+        return general_body(*args)
+
     return jax.shard_map(
         body, mesh=mesh, in_specs=placed, out_specs=P(("row", "col"), None), check_vma=False
     )

time: 132 us -> 28.2 us (0.21)
  blocking collectives: 47.4 us -> 0 us
  waiting for transfers between devices: 40 us -> 0 us
  Pallas kernels: 0 us -> 25.8 us
  between operations: 14.2 us -> 0.66 us
  local copies, waits for them, and re-layouts: 11.1 us -> 1.54 us
  matrix products: 8.67 us -> 0 us
  starting transfers between devices: 7.36 us -> 0 us
  other arithmetic: 3.09 us -> 0 us
    reduce_scatter x2 -> x0, waiting for transfers between devices: 40 us -> none  [couple(): lax.psum_scatter(flat_sum.astype(jnp.bfloat16), 'row', scatter_dimension=...]
    all_to_all x3 -> x0, blocking collectives: 34.8 us -> none  [the longest x2 25.3 us: body(): lax.all_to_all(coupled.astype(jnp.bfloat16), 'col', split_axis=0, concat_...]
    pallas_call x0 -> x1, Pallas kernels: none -> 25.8 us  [kernel_body(): pl.pallas_call(functools.partial(link_kernel, n_col, seats), out_shape=ja...]
    all_gather x2 -> x0, blocking collectives: 12.6 us -> none  [couple(): gathered = lax.all_gather(grid_mixed, 'row', axis=0, tiled=True)]
    dot_general x4 -> x0, matrix products: 8.67 us -> none  [the longest x2 6.72 us: seat_product(): jnp.einsum('skab,skbh->sah', seat_blocks, pieces, preferred_element_type=...]
    all_to_all x1 -> x0, starting transfers between devices: 7.28 us -> none  [to_grid(): lax.all_to_all(values, 'col', split_axis=0, concat_axis=0, tiled=True)]
    gather x2 -> x0, local copies, waits for them, and re-layouts: 5.3 us -> none  [seat_product(): pieces = pieces_all[seat_cols]]
    scatter x2 -> x0, local copies, waits for them, and re-layouts: 4.42 us -> none  [the longest x1 3.62 us: seat_layout(): seat_blocks = jnp.zeros((seat_total, block_len, block_len), blocks.dtype)...]
  transfers between devices with their start and end apart: 3 -> 0, of which waited for: 2 -> 0; matrix products, arithmetic and copies ran while one was open for 5% -> 0% of each run, Pallas kernels for 0% -> 0%
where the time goes in v1:
time: 28.2 us; the launch traced here: 28 us
  Pallas kernels  25.8 us (91%)
  local copies, waits for them, and re-layouts  1.54 us (5%)
  between operations  0.66 us (2%)
    pallas_call x1, Pallas kernels, kernel_body(): pl.pallas_call(functools.partial(link_kernel, n_col, seats), out_shape=ja...  25.8 us
    unnamed x1, local copies, waits for them, and re-layouts  1.54 us

profile of v1, /device:TPU:0, one launch (start us, length us, event | category | flops | bytes accessed | tf_op | source)
XLA Modules:
  0.0 28.0 jit_solution(12958911886590649854)
XLA Ops:
  0.7 25.8 %shard_map.82 = bf16[128,384]{1,0:T(8,128)(2,1)} custom-call(bf16[128,384]{1,0:T(8,128)(2,1)} %states.1, bf16[384,384]{1,0:T(8,128)(2,1)} %mix_weight.1, bf16[32,128,128]{2,1,0:T(8,128)(2,1)} %bitcast.3, s32[32]{0:T(128)} %bitcast.4, s32[32]{0:T(128)} %bitcast.5, s32[1,1]{1,0:T(1,128)S(6)} %copy.10.live_count_in, f32[384]{0:T(512)} %gain_in.1, f32[384]{0:T(512)} %bias_in.1), custom_call_target="tpu_custom_call" | custom-call | tf_op jit(solution)/shard_map/pallas_call | solution.py:376
  26.5 1.5 %copy.11 = bf16[128,384]{1,0:T(8,128)(2,1)} copy(bf16[128,384]{1,0:T(8,128)(2,1)} %shard_map.82) | data formatting | bytes 196608

commit v2 on v1

v2 whole, which is shorter than its diff:
```python
import functools

import jax
import jax.numpy as jnp
from jax import lax
from jax.experimental import pallas as pl
from jax.experimental.pallas import tpu as pltpu
from jax.sharding import PartitionSpec as P

ITERS = 2
ROW_TILE = 16
MESH_IDS = pl.DeviceIdType.MESH


def normalize(hidden, coupled, gain, bias):
    summed_in = hidden.astype(jnp.float32) + coupled
    mean_value = jnp.mean(summed_in, axis=-1, keepdims=True)
    centered = summed_in - mean_value
    variance = jnp.mean(centered * centered, axis=-1, keepdims=True)
    return (centered * lax.rsqrt(variance + 1e-05) * gain + bias).astype(jnp.bfloat16)


def to_grid(values):
    return lax.all_to_all(values, "col", split_axis=0, concat_axis=0, tiled=True)


def seat_layout(blocks, row_ids, col_ids, live_count, row_groups, seats_per_row):
    slot_total = row_ids.shape[0]
    block_len = blocks.shape[1]
    slot_ids = jnp.arange(slot_total, dtype=jnp.int32)
    live_mask = slot_ids < live_count
    earlier = (
        (row_ids[:, None] == row_ids[None, :])
        & (slot_ids[None, :] < slot_ids[:, None])
        & live_mask[None, :]
    )
    rank_in_row = jnp.sum(earlier.astype(jnp.int32), axis=1)
    seat_total = row_groups * seats_per_row
    seat_index = jnp.where(live_mask, row_ids * seats_per_row + rank_in_row, seat_total)
    seat_blocks = (
        jnp.zeros((seat_total, block_len, block_len), blocks.dtype)
        .at[seat_index]
        .set(blocks, mode="drop")
    )
    seat_cols = jnp.zeros((seat_total,), jnp.int32).at[seat_index].set(col_ids, mode="drop")
    return (
        seat_blocks.reshape(row_groups, seats_per_row, block_len, block_len),
        seat_cols.reshape(row_groups, seats_per_row),
    )


def couple(grid_mixed, prepared):
    gathered = lax.all_gather(grid_mixed, "row", axis=0, tiled=True)
    row_groups = lax.axis_size("row")
    block_len, feat_width = grid_mixed.shape
    pieces_all = gathered.reshape(row_groups, block_len, feat_width)
    seat_blocks, seat_cols = prepared
    chosen = (seat_cols[:, :, None] == jnp.arange(row_groups)).astype(grid_mixed.dtype)
    pieces = jnp.einsum(
        "skj,jbh->skbh", chosen, pieces_all, preferred_element_type=jnp.float32
    ).astype(grid_mixed.dtype)
    flat_sum = jnp.einsum(
        "skab,skbh->sah", seat_blocks, pieces, preferred_element_type=jnp.float32
    ).reshape(row_groups * block_len, feat_width)
    return lax.psum_scatter(
        flat_sum.astype(jnp.bfloat16), "row", scatter_dimension=0, tiled=True
    ).astype(jnp.float32)


def general_body(states, mix_weight, coherence, block_row, block_col, block_count, gain, bias):
    row_ids = block_row[0, 0]
    row_groups = lax.axis_size("row")
    slot_total = row_ids.shape[0]
    seats_per_row = max(2, (slot_total + row_groups - 1) // row_groups)
    prepared = seat_layout(
        coherence[0, 0], row_ids, block_col[0, 0], block_count[0, 0], row_groups, seats_per_row
    )
    hidden = to_grid(states)
    for iteration in range(ITERS):
        mixed = jnp.dot(hidden, mix_weight, preferred_element_type=jnp.float32).astype(jnp.bfloat16)
        hidden = normalize(hidden, couple(mixed, prepared), gain, bias)
    return to_grid(hidden)


def lowest_bit_index(bit):
    index = jnp.int32(0)
    for power, pattern in enumerate((-1431655766, -858993460, -252645136, -16711936, -65536)):
        index = index + jnp.where((bit & jnp.int32(pattern)) != 0, jnp.int32(1 << power), jnp.int32(0))
    return index


ORDER = (0, 2, 1, 3)


def link_kernel(
    n_col,
    seats,
    states,
    mix_weight,
    coherence,
    row_ids_in,
    col_ids_in,
    live_count_in,
    gain_in,
    bias_in,
    out,
    row_ids,
    col_ids,
    live_count,
    gain_row,
    bias_row,
    coh,
    weight,
    hall,
    hall2,
    fin,
    near_out,
    near_in,
    chip_sum,
    far_out,
    far_in,
    joint,
    load_sem,
    scatter_send,
    scatter_recv,
    pair_send,
    pair_recv,
    near_send,
    near_recv,
    far_send,
    far_recv,
    next_send,
    next_recv,
    back_send,
    back_recv,
):
    r = lax.axis_index("row")
    c = lax.axis_index("col")
    blk = hall.shape[0] // 4
    part = blk // n_col
    slots = coh.shape[0]
    mate = (r ^ 1, c)
    across = (r ^ 2, c)
    steps = tuple(range(n_col - 1, 0, -1))

    def remote(src, dst, send_sem, recv_sem, device):
        return pltpu.make_async_remote_copy(
            src_ref=src, dst_ref=dst, send_sem=send_sem, recv_sem=recv_sem,
            device_id=device, device_id_type=MESH_IDS,
        )

    def rows_at(index, size=part):
        return pl.ds(pl.multiple_of(index * size, size), size)

    barrier = pltpu.get_barrier_semaphore()
    for peer in (
        [(r ^ 2, c ^ step) for step in steps] + [(r, c ^ step) for step in steps] + [mate, across]
    ):
        pl.semaphore_signal(barrier, inc=1, device_id=peer, device_id_type=MESH_IDS)
    loads = [
        pltpu.make_async_copy(source, held, load_sem.at[4 + place])
        for place, (source, held) in enumerate(
            (
                (row_ids_in, row_ids),
                (col_ids_in, col_ids),
                (live_count_in, live_count),
                (gain_in, gain_row),
                (bias_in, bias_row),
            )
        )
    ]
    for load in loads[:3]:
        load.start()
    load_coh = pltpu.make_async_copy(coherence, coh, load_sem.at[0])
    load_weight = pltpu.make_async_copy(mix_weight, weight, load_sem.at[1])
    load_own = pltpu.make_async_copy(states.at[rows_at(c)], hall.at[rows_at(c)], load_sem.at[2])
    load_coh.start()
    load_own.start()
    load_weight.start()
    for load in loads[3:]:
        load.start()

    pl.semaphore_wait(barrier, 2 * n_col)

    over_rows = pl.ds(pl.multiple_of(blk + c * part, part), part)
    for step in steps + (0,):
        source = states.at[rows_at(c ^ step)]
        remote(
            source, hall.at[over_rows], scatter_send, scatter_recv.at[1], (r ^ 2, c ^ step)
        ).start()
        if step:
            remote(
                source, hall.at[rows_at(c)], scatter_send, scatter_recv.at[0], (r, c ^ step)
            ).start()

    def landed(low, size, send_sem, recv_sem):
        whole = hall.at[pl.ds(low, size)]
        return remote(whole, whole, send_sem, recv_sem, mate)

    for load in loads:
        load.wait()
    gain = gain_row[...].reshape(1, -1)
    bias = bias_row[...].reshape(1, -1)
    live = live_count[0, 0]
    row_bits = [jnp.int32(0)] * 4
    for k in range(slots):
        named = row_ids[k] ^ r
        bit = jnp.where(k < live, jnp.int32(1 << k if k < 31 else -(1 << 31)), jnp.int32(0))
        for q in range(4):
            row_bits[q] = row_bits[q] | jnp.where(named == q, bit, jnp.int32(0))
    load_coh.wait()

    def partial(q, reader, write):
        bits = row_bits[q]
        places, scales = [], []
        for n in range(seats):
            low = bits & (-bits)
            place = lowest_bit_index(low)
            named = jnp.where(low != 0, col_ids[place] ^ (r ^ reader), jnp.int32(-1))
            places.append(place)
            scales.append(
                [jnp.where(named == t, jnp.float32(1), jnp.float32(0)) for t in ORDER]
            )
            bits = bits & (bits - 1)
        size = 32

        def some_rows(i, carry):
            rows = rows_at(i, size)
            sums = [jnp.zeros((size, blk), jnp.float32)] * 4
            for n in range(seats):
                block = coh[places[n], rows, :].astype(jnp.float32)
                sums = [sums[t] + block * scales[n][t] for t in range(4)]
            for t in range(4):
                write(rows, t, sums[t])
            return carry

        lax.fori_loop(0, blk // size, some_rows, 0)

    def into(ref, half):
        def write(rows, t, values):
            ref[half, rows, t * blk : (t + 1) * blk] = values.astype(ref.dtype)

        return write

    near, far = [], []
    for half in range(2):
        partial((1, 3)[half], 1, into(near_out, half))
        near.append(
            remote(
                near_out.at[half], near_in.at[half],
                near_send.at[half], near_recv.at[half], mate,
            )
        )
        near[half].start()
    for half in range(2):
        partial((0, 2)[half], 0, into(chip_sum, half))
        near[half].wait_recv()
        chip_sum[half] = chip_sum[half] + near_in[half].astype(jnp.float32)
        far_out[half] = chip_sum[half].astype(far_out.dtype)
        far.append(
            remote(
                far_out.at[half], far_in.at[half], far_send.at[half], far_recv.at[half], across
            )
        )
        far[half].start()

    pairs = []
    load_own.wait()
    landed(0, blk - part, scatter_send, scatter_recv.at[0]).wait_recv()
    for half in range(2):
        if half:
            landed(0, blk, scatter_send, scatter_recv.at[1]).wait_recv()
        pairs.append(
            remote(
                hall.at[pl.ds(half * blk, blk)], hall.at[pl.ds((2 + half) * blk, blk)],
                pair_send.at[half], pair_recv.at[half], mate,
            )
        )
        pairs[half].start()
    load_weight.wait()

    for half in range(2):
        far[half].wait_recv()
        for t in range(4):
            mine = slice(t * blk, (t + 1) * blk)
            theirs = slice((t ^ 1) * blk, ((t ^ 1) + 1) * blk)
            joint[(1 - half) * blk : (2 - half) * blk, mine] = (
                chip_sum[1 - half, :, mine] + far_in[half, :, theirs].astype(jnp.float32)
            ).astype(joint.dtype)

    def product(rows, source, low, high):
        return jnp.dot(
            joint[rows, low * blk : high * blk], source[low * blk : high * blk, :],
            preferred_element_type=jnp.float32,
        )

    def settle(spread, rows, source):
        coupled = jnp.dot(
            spread.astype(jnp.bfloat16), weight[...], preferred_element_type=jnp.float32
        )
        return normalize(source[rows, :], coupled, gain, bias)

    halves = (slice(0, blk), slice(blk, 2 * blk))
    first = product(slice(0, 2 * blk), hall, 0, 2)
    for copy in pairs:
        copy.wait_recv()
    spread = first + product(slice(0, 2 * blk), hall, 2, 4)
    nexts = []
    for half, rows in enumerate(halves):
        hall2[rows, :] = settle(spread[rows], rows, hall)
        nexts.append(
            remote(
                hall2.at[pl.ds(half * blk, blk)], hall2.at[pl.ds((2 + half) * blk, blk)],
                next_send.at[half], next_recv.at[half], mate,
            )
        )
        nexts[half].start()
    first = product(halves[0], hall2, 0, 2)
    for copy in nexts:
        copy.wait_recv()
    fin[...] = settle(first + product(halves[0], hall2, 2, 4), halves[0], hall2)

    for step in steps:
        remote(
            fin.at[rows_at(c ^ step)], out.at[rows_at(c)], back_send, back_recv, (r, c ^ step)
        ).start()
    keep = pltpu.make_async_copy(fin.at[rows_at(c)], out.at[rows_at(c)], load_sem.at[3])
    keep.start()

    landed(0, 2 * blk - part, scatter_send, scatter_recv.at[0]).wait_send()
    for copy in near + far + pairs + nexts:
        copy.wait_send()
    keep.wait()
    returned = landed(0, blk - part, back_send, back_recv)
    returned.wait_recv()
    returned.wait_send()


def kernel_body(states, mix_weight, coherence, block_row, block_col, block_count, gain, bias):
    n_col = lax.axis_size("col")
    row_groups = lax.axis_size("row")
    blk, feat = states.shape
    slots = coherence.shape[2]
    seats = max(2, (slots + row_groups - 1) // row_groups)
    any_space = pl.BlockSpec(memory_space=pl.ANY)
    bf16, f32 = jnp.bfloat16, jnp.float32
    dma = pltpu.SemaphoreType.DMA
    wide = (2, blk, row_groups * blk)
    return pl.pallas_call(
        functools.partial(link_kernel, n_col, seats),
        out_shape=jax.ShapeDtypeStruct((blk, feat), bf16),
        in_specs=[any_space] * 8,
        out_specs=OUT_SPACE,
        scratch_shapes=[
            pltpu.SMEM((slots,), jnp.int32),
            pltpu.SMEM((slots,), jnp.int32),
            pltpu.SMEM((1, 1), jnp.int32),
            pltpu.VMEM((feat,), f32),
            pltpu.VMEM((feat,), f32),
            pltpu.VMEM((slots, blk, blk), bf16),
            pltpu.VMEM((feat, feat), bf16),
            pltpu.VMEM((row_groups * blk, feat), bf16),
            pltpu.VMEM((row_groups * blk, feat), bf16),
            pltpu.VMEM((blk, feat), bf16),
            pltpu.VMEM(wide, bf16),
            pltpu.VMEM(wide, bf16),
            pltpu.VMEM(wide, f32),
            pltpu.VMEM(wide, bf16),
            pltpu.VMEM(wide, bf16),
            pltpu.VMEM((2 * blk, row_groups * blk), bf16),
            dma((9,)),
            dma,
            dma((2,)),
        ]
        + [dma((2,))] * 8
        + [dma] * 2,
        compiler_params=pltpu.CompilerParams(
            collective_id=0, has_side_effects=True, vmem_limit_bytes=60 << 20
        ),
    )(
        states,
        mix_weight,
        coherence.reshape(coherence.shape[2:]),
        block_row.reshape(slots),
        block_col.reshape(slots),
        block_count,
        gain,
        bias,
    )


OUT_SPACE = pl.BlockSpec(memory_space=pltpu.VMEM)


def solution(mesh):
    placed = (
        P(("row", "col"), None),
        P(),
        P("row", "col", None, None, None),
        P("row", "col", None),
        P("row", "col", None),
        P("row", "col"),
        P(),
        P(),
    )
    n_row, n_col = mesh.shape["row"], mesh.shape["col"]

    def body(*args):
        blk = args[0].shape[0]
        slots = args[2].shape[2]
        in_tiles = blk % n_col == 0 and (blk // n_col) % ROW_TILE == 0
        pairs_up = n_col > 1 and n_col & (n_col - 1) == 0
        if n_row == 4 and pairs_up and in_tiles and slots <= 32:
            return kernel_body(*args)
        return general_body(*args)

    return jax.shard_map(
        body, mesh=mesh, in_specs=placed, out_specs=P(("row", "col"), None), check_vma=False
    )
```

time: 28.2 us -> 26.7 us (0.947)
  Pallas kernels: 25.8 us -> 24.3 us
    pallas_call x1, Pallas kernels: 25.8 us -> 24.3 us  [kernel_body(): pl.pallas_call(functools.partial(link_kernel, n_col, seats), out_shape=ja...]
where the time goes in v2:
time: 26.7 us; the launch traced here: 26.5 us
  Pallas kernels  24.3 us (91%)
  local copies, waits for them, and re-layouts  1.54 us (6%)
  between operations  0.66 us (2%)
    pallas_call x1, Pallas kernels, kernel_body(): pl.pallas_call(functools.partial(link_kernel, n_col, seats), out_shape=ja...  24.3 us
    unnamed x1, local copies, waits for them, and re-layouts  1.54 us

profile of v2, /device:TPU:0, one launch (start us, length us, event | category | flops | bytes accessed | tf_op | source)
XLA Modules:
  0.0 26.5 jit_solution(11330553723663088399)
XLA Ops:
  0.7 24.3 %shard_map.82 = bf16[128,384]{1,0:T(8,128)(2,1)} custom-call(bf16[128,384]{1,0:T(8,128)(2,1)} %states.1, bf16[384,384]{1,0:T(8,128)(2,1)} %mix_weight.1, bf16[32,128,128]{2,1,0:T(8,128)(2,1)} %bitcast.3, s32[32]{0:T(128)} %bitcast.4, s32[32]{0:T(128)} %bitcast.5, s32[1,1]{1,0:T(1,128)S(6)} %copy.10.live_count_in, f32[384]{0:T(512)} %gain_in.1, f32[384]{0:T(512)} %bias_in.1), custom_call_target="tpu_custom_call" | custom-call | tf_op jit(solution)/shard_map/pallas_call | solution.py:349
  25.0 1.5 %copy.11 = bf16[128,384]{1,0:T(8,128)(2,1)} copy(bf16[128,384]{1,0:T(8,128)(2,1)} %shard_map.82) | data formatting | bytes 196608

commit v3 on v2

--- a/solution.py
+++ b/solution.py
@@ -252,7 +252,6 @@
             )
         )
         near[half].start()
-    for half in range(2):
         partial((0, 2)[half], 0, into(chip_sum, half))
         near[half].wait_recv()
         chip_sum[half] = chip_sum[half] + near_in[half].astype(jnp.float32)

time: 26.7 us -> 26.5 us (level)
  no operation moved by 1% of the time
where the time goes in v3:
time: 26.5 us; the launch traced here: 26.3 us
  Pallas kernels  24.1 us (91%)
  local copies, waits for them, and re-layouts  1.54 us (6%)
  between operations  0.66 us (2%)
    pallas_call x1, Pallas kernels, kernel_body(): pl.pallas_call(functools.partial(link_kernel, n_col, seats), out_shape=ja...  24.1 us
    unnamed x1, local copies, waits for them, and re-layouts  1.54 us

profile of v3, /device:TPU:0, one launch (start us, length us, event | category | flops | bytes accessed | tf_op | source)
XLA Modules:
  0.0 26.3 jit_solution(13328644623775786130)
XLA Ops:
  0.7 24.1 %shard_map.82 = bf16[128,384]{1,0:T(8,128)(2,1)} custom-call(bf16[128,384]{1,0:T(8,128)(2,1)} %states.1, bf16[384,384]{1,0:T(8,128)(2,1)} %mix_weight.1, bf16[32,128,128]{2,1,0:T(8,128)(2,1)} %bitcast.3, s32[32]{0:T(128)} %bitcast.4, s32[32]{0:T(128)} %bitcast.5, s32[1,1]{1,0:T(1,128)S(6)} %copy.10.live_count_in, f32[384]{0:T(512)} %gain_in.1, f32[384]{0:T(512)} %bias_in.1), custom_call_target="tpu_custom_call" | custom-call | tf_op jit(solution)/shard_map/pallas_call | solution.py:348
  24.8 1.5 %copy.11 = bf16[128,384]{1,0:T(8,128)(2,1)} copy(bf16[128,384]{1,0:T(8,128)(2,1)} %shard_map.82) | data formatting | bytes 196608
